TPU v7x, 32 devices: a whole 2x2x4 slice. The times are simulated.
32 devices in a mesh: row: 4 (over z), col: 4 (over y, x), ch: 2 (over core).
Axes of the slice: x: 2, y: 2, z: 4, core: 2. Of those that a mesh axis runs over, the one named last changes fastest.
Arguments:
- field: float32 [32, 512, 2048], P(None, 'row', 'col'), may hold values from -6 to 6
- spec_weight: float32 [2, 32, 32, 512], replicated, may hold values from -0.75 to 0.75
- point_weight: float32 [32, 32], replicated, may hold values from -1 to 1
- bias: float32 [32], P('ch'), may hold values from -1 to 1
- kept_modes: int32 [32], replicated, may hold values from 8 to 16, as said below
- residual: float32 [32, 16384], P('ch', ('row', 'col')), may hold values from -6 to 6
- trace_dest: int32 [16384, 1], P(('row', 'col')), may hold values from 0 to 15; in each aligned block of 1024 rows (0 to 1023, 1024 to 2047, ...) at most 128 rows name the same one
- trace_cell: int32 [16384], P(('row', 'col')), may hold values from 0 to 65535
Outputs:
- grad_field: float32 [32, 512, 2048], P('ch', 'row', 'col')
- grad_spec: float32 [2, 32, 32, 512], P(None, None, 'ch')
- grad_point: float32 [32, 32], P(None, 'ch')
- grad_bias: float32 [32], P('ch')
Inputs may be any that keep to these rules, and one draw needn't show every extreme that they name: `trace_dest`: of the 1024 points of one device, at most 128 go to one tile. `kept_modes`: some channel keeps 16 and some keeps 16 // 2.
All inputs are finite; a program needn't handle non-finite values.
Results may differ from a plain program's by a relative error of at most 0.00012.
Values sent between devices are 32-bit elements; how exact they have to be, the bound alone decides.
A program may use at most 192 MiB of HBM per device.

v0:
```python
import math
import jax
import jax.numpy as jnp
from jax import lax
from jax.sharding import PartitionSpec as P

C = 32
M = 16
RD = 128
CD = 512
P_DEV = 1024
MODES = 512
full_turn = 6.283185307179586
exact_mode = lax.Precision.HIGHEST


def row_angles(start_at, extent, period):
    frequency = jnp.arange(2 * M, dtype=jnp.int32)
    frequency = jnp.where(frequency < M, frequency, frequency - 2 * M)
    places = start_at + jnp.arange(extent, dtype=jnp.int32)
    phases = frequency[:, None] * places[None, :] % period
    angles = phases.astype(jnp.float32) * (full_turn / period)
    return (jnp.cos(angles), jnp.sin(angles))


def col_angles(start_at, extent, period):
    frequency = jnp.arange(M, dtype=jnp.int32)
    places = start_at + jnp.arange(extent, dtype=jnp.int32)
    phases = places[:, None] * frequency[None, :] % period
    angles = phases.astype(jnp.float32) * (full_turn / period)
    return (jnp.cos(angles), jnp.sin(angles))


def mode_mask(kept_modes):
    indices = jnp.arange(MODES, dtype=jnp.int32)
    row_mode = indices // M
    col_mode = indices % M
    row_rank = jnp.where(row_mode < M, row_mode, 2 * M - 1 - row_mode)
    allowed = (row_rank[None, :] < kept_modes[:, None]) & (col_mode[None, :] < kept_modes[:, None])
    return allowed.astype(jnp.float32)


def widen(values, full_size, along):
    shape_full = list(values.shape)
    block_size = values.shape[along]
    shape_full[along] = full_size
    holder = jnp.zeros(tuple(shape_full), jnp.float32)
    return lax.dynamic_update_slice_in_dim(holder, values, lax.axis_index("ch") * block_size, along)


def local_modes(own_field, scale_by):
    channel_count, row_count, col_count = own_field.shape
    row_devices = lax.axis_size("row")
    height = row_count * row_devices
    breadth = col_count * lax.axis_size("col")
    row_place = lax.axis_index("row")
    cos_rows, sin_rows = row_angles(row_place * row_count, row_count, height)
    real_rows = jnp.einsum("ar,crs->cas", cos_rows, own_field, precision=exact_mode)
    imag_rows = -jnp.einsum("ar,crs->cas", sin_rows, own_field, precision=exact_mode)
    col_first = lax.axis_index("col") * col_count
    cos_cols, sin_cols = col_angles(col_first, col_count, breadth)
    mode_re = jnp.einsum("cas,sb->cab", real_rows, cos_cols, precision=exact_mode) + jnp.einsum(
        "cas,sb->cab", imag_rows, sin_cols, precision=exact_mode
    )
    mode_im = jnp.einsum("cas,sb->cab", imag_rows, cos_cols, precision=exact_mode) - jnp.einsum(
        "cas,sb->cab", real_rows, sin_cols, precision=exact_mode
    )
    return (
        mode_re.reshape(channel_count, MODES) * scale_by,
        mode_im.reshape(channel_count, MODES) * scale_by,
    )


def tile_field(mode_re, mode_im, scale_by):
    channel_count = mode_re.shape[0]
    grid_re = mode_re.reshape(channel_count, 2 * M, M)
    grid_im = mode_im.reshape(channel_count, 2 * M, M)
    height = RD * lax.axis_size("row")
    breadth = CD * lax.axis_size("col")
    cos_cols, sin_cols = col_angles(lax.axis_index("col") * CD, CD, breadth)
    half_re = jnp.einsum("cab,sb->cas", grid_re, cos_cols, precision=exact_mode) - jnp.einsum(
        "cab,sb->cas", grid_im, sin_cols, precision=exact_mode
    )
    half_im = jnp.einsum("cab,sb->cas", grid_re, sin_cols, precision=exact_mode) + jnp.einsum(
        "cab,sb->cas", grid_im, cos_cols, precision=exact_mode
    )
    cos_rows, sin_rows = row_angles(lax.axis_index("row") * RD, RD, height)
    result = jnp.einsum("ar,cas->crs", cos_rows, half_re, precision=exact_mode) - jnp.einsum(
        "ar,cas->crs", sin_rows, half_im, precision=exact_mode
    )
    return result * scale_by


def per_device(
    field, spec_weight, point_weight, bias, kept_modes, residual, trace_dest, trace_cell
):
    channel_count = C // lax.axis_size("ch")
    own_first = lax.axis_index("ch") * channel_count
    row_devices = lax.axis_size("row")
    col_devices = lax.axis_size("col")
    tiles_all = row_devices * col_devices
    points_all = P_DEV * tiles_all
    capacity = max(2, 2 * P_DEV // tiles_all)
    forward_scale = 1.0 / math.sqrt(RD * row_devices * CD * col_devices)
    mix_scale = 1.0 / math.sqrt(MODES)
    own_field = lax.dynamic_slice_in_dim(field, own_first, channel_count, 0)
    part_re, part_im = local_modes(own_field, forward_scale)
    spec_re, spec_im = lax.psum((widen(part_re, C, 0), widen(part_im, C, 0)), ("row", "col", "ch"))
    allowed = mode_mask(kept_modes)
    weight_re = spec_weight[0] * allowed[None, :, :]
    weight_im = spec_weight[1] * allowed[None, :, :]
    out_wre = lax.dynamic_slice_in_dim(weight_re, own_first, channel_count, 1)
    out_wim = lax.dynamic_slice_in_dim(weight_im, own_first, channel_count, 1)
    mixed_re = jnp.sum(out_wre * spec_re[:, None, :] - out_wim * spec_im[:, None, :], axis=0)
    mixed_im = jnp.sum(out_wre * spec_im[:, None, :] + out_wim * spec_re[:, None, :], axis=0)
    out_point = lax.dynamic_slice_in_dim(point_weight, own_first, channel_count, 1)
    pre_act = (
        tile_field(mixed_re, mixed_im, mix_scale)
        + jnp.einsum("co,crs->ors", out_point, field, precision=exact_mode)
        + bias[:, None, None]
    )
    targets = trace_dest[:, 0]
    one_hot = (targets[:, None] == jnp.arange(tiles_all, dtype=jnp.int32)[None, :]).astype(
        jnp.int32
    )
    earlier = jnp.cumsum(one_hot, axis=0) - one_hot
    slot_rank = jnp.sum(earlier * one_hot, axis=1)
    position = targets * capacity + slot_rank
    send_values = (
        jnp.zeros((channel_count, tiles_all * capacity), jnp.float32).at[:, position].set(residual)
    )
    send_cells = jnp.zeros((tiles_all * capacity,), jnp.int32).at[position].set(trace_cell)
    got_values, got_cells = (
        lax.all_to_all(
            send_values.reshape(channel_count, tiles_all, capacity),
            ("row", "col"),
            split_axis=1,
            concat_axis=1,
            tiled=True,
        ),
        lax.all_to_all(
            send_cells.reshape(1, tiles_all, capacity),
            ("row", "col"),
            split_axis=1,
            concat_axis=1,
            tiled=True,
        ),
    )
    cotangent = (
        jnp.zeros((channel_count, RD * CD), jnp.float32)
        .at[:, got_cells.reshape(-1)]
        .add(got_values.reshape(channel_count, -1))
    )
    cotangent = cotangent.reshape(channel_count, RD, CD)
    out_slope = jax.vjp(jax.nn.gelu, pre_act)[1](cotangent)[0]
    grad_re, grad_im = local_modes(out_slope, mix_scale)
    point_part = jnp.einsum("crs,ors->co", field, out_slope, precision=exact_mode)
    bias_part = jnp.sum(out_slope, axis=(1, 2))
    modes_re, modes_im, point_sum, bias_sum = lax.psum(
        (
            widen(grad_re, C, 0),
            widen(grad_im, C, 0),
            widen(point_part, C, 1),
            widen(bias_part, C, 0),
        ),
        ("row", "col", "ch"),
    )
    own_allowed = lax.dynamic_slice_in_dim(allowed, own_first, channel_count, 0)
    own_gre = lax.dynamic_slice_in_dim(modes_re, own_first, channel_count, 0)
    own_gim = lax.dynamic_slice_in_dim(modes_im, own_first, channel_count, 0)
    grad_scale = math.sqrt(MODES / points_all)
    spec_grad_re = (
        own_allowed[None]
        * (own_gre[None] * spec_re[:, None] + own_gim[None] * spec_im[:, None])
        * grad_scale
    )
    spec_grad_im = (
        own_allowed[None]
        * (own_gim[None] * spec_re[:, None] - own_gre[None] * spec_im[:, None])
        * grad_scale
    )
    grad_spec = jnp.stack((spec_grad_re, spec_grad_im), axis=0)
    in_wre = lax.dynamic_slice_in_dim(weight_re, own_first, channel_count, 0)
    in_wim = lax.dynamic_slice_in_dim(weight_im, own_first, channel_count, 0)
    adjoint_re = jnp.sum(in_wre * modes_re[None] + in_wim * modes_im[None], axis=1)
    adjoint_im = jnp.sum(in_wre * modes_im[None] - in_wim * modes_re[None], axis=1)
    spectral_back = tile_field(adjoint_re, adjoint_im, forward_scale)
    own_point = lax.dynamic_slice_in_dim(point_weight, own_first, channel_count, 1)
    partial_back = jnp.einsum("co,ors->crs", own_point, out_slope, precision=exact_mode)
    point_back = lax.psum_scatter(partial_back, "ch", scatter_dimension=0, tiled=True)
    grad_field = point_back + spectral_back
    norm_points = 1.0 / math.sqrt(points_all)
    grad_point = lax.dynamic_slice_in_dim(point_sum, own_first, channel_count, 1) * norm_points
    grad_bias = lax.dynamic_slice_in_dim(bias_sum, own_first, channel_count, 0) * norm_points
    return (grad_field, grad_spec, grad_point, grad_bias)


def solution(mesh):
    return jax.shard_map(
        per_device,
        mesh=mesh,
        in_specs=(
            P(None, "row", "col"),
            P(),
            P(),
            P("ch"),
            P(),
            P("ch", ("row", "col")),
            P(("row", "col"), None),
            P(("row", "col")),
        ),
        out_specs=(P("ch", "row", "col"), P(None, None, "ch", None), P(None, "ch"), P("ch")),
        check_vma=False,
    )
```

profile of v0, /device:TPU:0, one launch (start us, length us, event | category | flops | bytes accessed | tf_op | source)
XLA Modules:
  0.0 457.2 jit_solution(12711133566505198467)
XLA Ops:
  7.9 4.5 reduce-window.6
  14.2 5.0 %scatter_custom_fusion = s32[2048]{0:T(1024)} fusion(s32[1024]{0:T(1024)S(1)} %bitcast.156, s32[1024]{0:T(1024)} %param.15, s32[]{:T(128)} %constant.114.clone.1), kind=kCustom, calls=%fused_computation.137 | custom fusion | bytes 8704 | tf_op jit(solution)/shard_map/scatter | solution.py:132
  19.3 8.3 %all-to-all-start = ((s32[1,16,128]{2,0,1:T(1,128)}), s32[1,16,128]{2,0,1:T(1,128)S(1)}, u32[]{:S(2)}, u32[]{:S(2)}) async-start(s32[1,16,128]{2,0,1:T(1,128)} %bitcast.7), calls=%async_computation | async-start | bytes 16384 | tf_op jit(solution)/shard_map/all_to_all | solution.py:141
  27.7 4.4 fusion.23
  32.1 4.4 fusion.17
  40.9 2.2 fusion.28
  46.8 14.1 %fusion.4 = f32[16,128,512]{2,0,1:T(8,128)} fusion(f32[32,128,512]{2,1,0:T(8,128)} %param.8, f32[32,32]{1,0:T(8,128)S(1)} %copy-done, s32[]{:T(128)S(6)} %select_n.97), kind=kOutput, calls=%fused_computation.7 | convolution fusion | flops 402653184 | bytes 12587012 | tf_op jit(solution)/shard_map/co,crs->ors/dot_general | solution.py:119
  64.1 3.7 scatter_custom_fusion.1
  68.8 5.3 %copy.92 = f32[16,128,512]{1,2,0:T(8,128)} copy(f32[16,128,512]{2,0,1:T(8,128)} %fusion.4) | data formatting | bytes 8388608 | tf_op jit(solution)/shard_map/co,crs->ors/dot_general | solution.py:119
  74.1 7.0 %all-to-all-start.1 = ((f32[16,16,128]{2,0,1:T(8,128)}), f32[16,16,128]{2,0,1:T(8,128)}, u32[]{:S(2)}, u32[]{:S(2)}) async-start(f32[16,16,128]{2,0,1:T(8,128)} %copy.81), calls=%async_computation.1 | async-start | bytes 262144 | tf_op jit(solution)/shard_map/all_to_all | solution.py:134
  81.1 90.1 %all-reduce.8.cloned.1.call-done = (f32[32,512]{1,0:T(8,128)}, f32[32,512]{1,0:T(8,128)}) async-done(((f32[32,512]{1,0:T(8,128)}, f32[32,512]{1,0:T(8,128)}), (f32[32,512]{1,0:T(8,128)}, f32[32,512]{1,0:T(8,128)})) %all-reduce.8.cloned.1.call-update) | async-done | bytes 131088 | tf_op jit(solution)/shard_map/psum | solution.py:108
  176.2 2.3 convolution_subtract_fusion.1
  178.5 8.7 %fusion.87 = f32[16,512,128]{2,1,0:T(8,128)} fusion(f32[16,32,512]{2,1,0:T(8,128)S(1)} %convolution_subtract_fusion.1, s32[128]{0:T(128)S(1)} %iota_add_fusion.1, s32[32]{0:T(128)S(1)} %compare_select_fusion.3), kind=kOutput, calls=%fused_computation.119 | convolution fusion | flops 402710528 | bytes 5243520 | tf_op jit(solution)/shard_map/ar,cas->crs/dot_general | solution.py:88
  190.5 26.2 %scatter_custom_fusion.2 = f32[16,65536]{0,1:T(8,128)} fusion(s32[2048]{0:T(1024)S(1)} %bitcast.155, f32[2048,16]{1,0:T(8,128)S(1)} %copy.83, f32[]{:T(128)} %constant.118.clone.1), kind=kCustom, calls=%fused_computation.3 | custom fusion | flops 32768 | bytes 4194308 | tf_op jit(solution)/shard_map/scatter-add | solution.py:152
  216.7 19.4 %copy.93 = f32[16,128,512]{1,2,0:T(8,128)} copy(f32[16,128,512]{0,2,1:T(8,128)} %bitcast.147) | data formatting | bytes 8388608 | tf_op jit(solution)/shard_map/reshape | solution.py:154
  236.1 14.2 %fusion.227 = (f32[16]{0:T(128)S(1)}, f32[16,128,512]{1,2,0:T(8,128)}) fusion(f32[16,128,512]{1,2,0:T(8,128)} %copy.93, f32[16]{0:T(128)S(1)} %copy-done.14, f32[16,128,512]{1,2,0:T(8,128)} %copy.92, f32[16,512,128]{2,1,0:T(8,128)} %fusion.87, f32[16,32,512]{2,1,0:T(8,128)S(1)} %copy-done.3, s32[128]{0:T(128)S(1)} %iota_add_fusion.1, ...), kind=kOutput, calls=%fused_computation.252 | convolution fusion | flops 427876352 | bytes 17826560 | tf_op jit(solution)/shard_map/ar,cas->crs/dot_general | solution.py:88
  250.4 5.5 %copy.95 = f32[16,128,512]{2,0,1:T(8,128)} copy(f32[16,128,512]{1,2,0:T(8,128)} %get-tuple-element.35) | data formatting | bytes 8388608 | tf_op jit(solution)/shard_map/transpose(jvp())/add_any | solution.py:155
  255.9 6.8 %fusion.26 = f32[16,32,512]{2,1,0:T(8,128)S(1)} fusion(f32[16,128,512]{1,2,0:T(8,128)} %get-tuple-element.35, s32[128]{0:T(128)S(1)} %iota_add_fusion.1, s32[32]{0:T(128)S(1)} %compare_select_fusion.3), kind=kOutput, calls=%fused_computation.31 | convolution fusion | flops 402972672 | bytes 5243520 | tf_op jit(solution)/shard_map/ar,crs->cas/dot_general | solution.py:59
  262.7 4.6 convolution_bitcast_fusion
  269.5 2.9 fusion.61
  272.4 2.9 fusion.30
  276.5 3.1 fusion.29
  280.7 11.0 %fusion.77 = f32[32,128,512]{2,0,1:T(8,128)} fusion(f32[16,128,512]{2,0,1:T(8,128)} %copy.95, f32[32,32]{1,0:T(8,128)S(1)} %copy-done, s32[]{:T(128)S(6)} %select_n.97), kind=kOutput, calls=%fused_computation.109 | convolution fusion | flops 402653184 | bytes 12587012 | tf_op jit(solution)/shard_map/co,ors->crs/dot_general | solution.py:189
  292.0 14.4 %fusion.34 = f32[32,32]{0,1:T(8,128)S(1)} fusion(f32[32,32]{0,1:T(8,128)S(1)} %broadcast_in_dim.10, s32[]{:T(128)S(6)} %select_n.97, f32[16,128,512]{2,0,1:T(8,128)} %copy.95, f32[32,128,512]{2,1,0:T(8,128)} %param.8), kind=kOutput, calls=%fused_computation.46 | convolution fusion | flops 402653184 | bytes 12591108 | tf_op jit(solution)/shard_map/crs,ors->co/dot_general | solution.py:157
  306.4 40.2 %all-reduce = (f32[32,32]{0,1:T(8,128)S(1)}, f32[32]{0:T(128)S(1)}) all-reduce(f32[32,32]{0,1:T(8,128)S(1)} %fusion.34, f32[32]{0:T(128)S(1)} %dynamic_update_slice.23), channel_id=1, replica_groups=mesh['row'=4,'col'=4,'ch'=2] {'row','col','ch'}, use_global_device_ids=true, to_apply=%region_15.16 | all-reduce | flops 1056 | bytes 8448 | tf_op jit(solution)/shard_map/psum | solution.py:159
  347.8 55.3 %all-reduce.6.cloned.1.call-done = (f32[32,512]{1,0:T(8,128)}, f32[32,512]{1,0:T(8,128)}) async-done(((f32[32,512]{1,0:T(8,128)}, f32[32,512]{1,0:T(8,128)}), (f32[32,512]{1,0:T(8,128)}, f32[32,512]{1,0:T(8,128)})) %all-reduce.6.cloned.1.call-update) | async-done | bytes 131088 | tf_op jit(solution)/shard_map/psum | solution.py:159
  407.2 8.3 %fusion.84 = f32[16,512,128]{2,1,0:T(8,128)} fusion(f32[16,32,512]{2,1,0:T(8,128)S(1)} %convolution_subtract_fusion, s32[128]{0:T(128)S(1)} %iota_add_fusion.1, s32[32]{0:T(128)S(1)} %compare_select_fusion.3), kind=kOutput, calls=%fused_computation.116 | convolution fusion | flops 402710528 | bytes 5243520 | tf_op jit(solution)/shard_map/ar,cas->crs/dot_general | solution.py:88
  415.5 6.0 %copy.104 = f32[16,512,128]{1,0,2:T(8,128)} copy(f32[16,512,128]{2,1,0:T(8,128)} %fusion.84) | data formatting | bytes 8388608 | tf_op jit(solution)/shard_map/ar,cas->crs/dot_general | solution.py:88
  423.7 8.5 %fusion.79 = f32[16,512,128]{2,1,0:T(8,128)} fusion(f32[16,32,512]{2,1,0:T(8,128)S(1)} %convolution_add_fusion, s32[128]{0:T(128)S(1)} %iota_add_fusion.1, s32[32]{0:T(128)S(1)} %compare_select_fusion.3), kind=kOutput, calls=%fused_computation.111 | convolution fusion | flops 402710528 | bytes 5243520 | tf_op jit(solution)/shard_map/ar,cas->crs/dot_general | solution.py:88
  432.2 5.5 %copy.105 = f32[16,512,128]{1,0,2:T(8,128)} copy(f32[16,512,128]{2,1,0:T(8,128)} %fusion.79) | data formatting | bytes 8388608 | tf_op jit(solution)/shard_map/ar,cas->crs/dot_general | solution.py:88
  439.8 6.2 %bitcast_add_fusion = f32[16,128,512]{2,0,1:T(8,128)S(1)} fusion(f32[16,128,512]{2,0,1:T(8,128)} %reduce-scatter.2.cloned.1.call-done, f32[16,512,128]{1,0,2:T(8,128)} %copy.104, f32[16,512,128]{1,0,2:T(8,128)} %copy.105), kind=kLoop, calls=%fused_computation.17 | loop fusion | flops 3145728 | bytes 16777216 | tf_op jit(solution)/shard_map/add | solution.py:191
  446.0 4.4 copy.108
  (102 shorter events, 37.0 us)
Async XLA Ops:
  7.2 39.6 %copy-start = (f32[32,32]{1,0:T(8,128)S(1)}, f32[32,32]{1,0:T(8,128)}, u32[]{:S(2)}) copy-start(f32[32,32]{1,0:T(8,128)} %param.10) | copy-start | bytes 12292
  19.3 54.8 %all-to-all-start = ((s32[1,16,128]{2,0,1:T(1,128)}), s32[1,16,128]{2,0,1:T(1,128)S(1)}, u32[]{:S(2)}, u32[]{:S(2)}) async-start(s32[1,16,128]{2,0,1:T(1,128)} %bitcast.7), calls=%async_computation | async-start | bytes 16384 | tf_op jit(solution)/shard_map/all_to_all | solution.py:141
  27.6 143.7 %all-reduce.8.cloned.1.call-start = ((), (), s32[]{:S(2)}) async-start(), calls=%async_computation.5 | async-start | bytes 262144 | tf_op jit(solution)/shard_map/psum | solution.py:108
  46.1 0.6 copy-start.6
  46.1 0.6 copy-start.7
  46.8 14.2 %copy-start.13 = (s32[32]{0:T(128)S(1)}, s32[32]{0:T(128)}, u32[]{:S(2)}) copy-start(s32[32]{0:T(128)} %param.12) | copy-start | bytes 388
  46.8 14.2 %copy-start.2 = (f32[2,32,32,512]{3,2,1,0:T(8,128)S(1)}, f32[2,32,32,512]{3,2,1,0:T(8,128)}, u32[]{:S(2)}) copy-start(f32[2,32,32,512]{3,2,1,0:T(8,128)} %param.9) | copy-start | bytes 12582916
  61.0 2.1 copy-start.12
  74.1 115.2 %all-to-all-start.1 = ((f32[16,16,128]{2,0,1:T(8,128)}), f32[16,16,128]{2,0,1:T(8,128)}, u32[]{:S(2)}, u32[]{:S(2)}) async-start(f32[16,16,128]{2,0,1:T(8,128)} %copy.81), calls=%async_computation.1 | async-start | bytes 262144 | tf_op jit(solution)/shard_map/all_to_all | solution.py:134
  81.1 322.0 %all-reduce.6.cloned.1.call-start = ((), (), s32[]{:S(2)}) async-start(), calls=%async_computation.4 | async-start | bytes 262144 | tf_op jit(solution)/shard_map/psum | solution.py:159
  216.7 19.5 %copy-start.3 = (f32[16,32,512]{2,1,0:T(8,128)S(1)}, f32[16,32,512]{2,1,0:T(8,128)}, u32[]{:S(2)}) copy-start(f32[16,32,512]{2,1,0:T(8,128)} %convolution_add_fusion.1) | copy-start | bytes 3145732
  216.7 19.5 %copy-start.14 = (f32[16]{0:T(128)S(1)}, f32[16]{0:T(128)}, u32[]{:S(2)}) copy-start(f32[16]{0:T(128)} %param.11) | copy-start | bytes 196
  255.9 6.8 %copy-start.1 = (f32[16,128,512]{1,2,0:T(8,128)S(1)}, f32[16,128,512]{1,2,0:T(8,128)}, u32[]{:S(2)}) copy-start(f32[16,128,512]{1,2,0:T(8,128)} %get-tuple-element.35) | copy-start | bytes 12582916
  279.9 0.6 copy-start.8
  280.0 0.6 copy-start.9
  280.6 159.2 %reduce-scatter.2.cloned.1.call-start = ((), (), s32[]{:S(2)}) async-start(), calls=%async_computation.3 | async-start | bytes 12582912 | tf_op jit(solution)/shard_map/reduce_scatter | solution.py:190
  432.2 5.6 %copy-start.11 = (f32[32,512]{1,0:T(8,128)S(1)}, f32[32,512]{1,0:T(8,128)}, u32[]{:S(2)}) copy-start(f32[32,512]{1,0:T(8,128)} %get-tuple-element.26) | copy-start | bytes 196612
  432.2 5.6 %copy-start.10 = (f32[32,512]{1,0:T(8,128)S(1)}, f32[32,512]{1,0:T(8,128)}, u32[]{:S(2)}) copy-start(f32[32,512]{1,0:T(8,128)} %get-tuple-element.27) | copy-start | bytes 196612
  432.2 5.6 %copy-start.4 = (f32[32,512]{1,0:T(8,128)S(1)}, f32[32,512]{1,0:T(8,128)}, u32[]{:S(2)}) copy-start(f32[32,512]{1,0:T(8,128)} %get-tuple-element.28) | copy-start | bytes 196612
  432.2 5.6 %copy-start.5 = (f32[32,512]{1,0:T(8,128)S(1)}, f32[32,512]{1,0:T(8,128)}, u32[]{:S(2)}) copy-start(f32[32,512]{1,0:T(8,128)} %get-tuple-element.29) | copy-start | bytes 196612
Sparse Core Ops, SparseCore 0:
  46.9 124.3 all-reduce.7
  280.7 122.2 all-reduce.5
  405.4 15.7 reduce-scatter.1
where the time goes:
time: 465 us; the launch traced here: 457 us
  waiting for transfers between devices  145 us (31%)
  matrix products  131 us (28%)
  local copies, waits for them, and re-layouts  62.7 us (13%)
  other arithmetic  47.6 us (10%)
  blocking collectives  40.2 us (9%)
  starting transfers between devices  15.4 us (3%)
  between operations  14.5 us (3%)
    psum x1, waiting for transfers between devices, per_device(): lax.psum((widen(part_re, C, 0), widen(part_im, C, 0)), ('row', 'col', 'ch'))  90.1 us
    psum x1, waiting for transfers between devices, per_device(): lax.psum((widen(grad_re, C, 0), widen(grad_im, C, 0), widen(point_part, C...  55.3 us
    psum x1, blocking collectives, per_device(): lax.psum((widen(grad_re, C, 0), widen(grad_im, C, 0), widen(point_part, C...  40.2 us
    scatter-add x1, other arithmetic, per_device(): cotangent = jnp.zeros((channel_count, RD * CD), jnp.float32).at[:, got_ce...  26.2 us
    dot_general x2, matrix products, tile_field(): jnp.einsum('ar,cas->crs', sin_rows, half_im, precision=exact_mode)  22.7 us
    reshape x1, local copies, waits for them, and re-layouts, per_device(): cotangent = cotangent.reshape(channel_count, RD, CD)  19.4 us
    dot_general x2, matrix products, tile_field(): jnp.einsum('ar,cas->crs', cos_rows, half_re, precision=exact_mode)  17 us
    dot_general x1, matrix products, per_device(): jnp.einsum('crs,ors->co', field, out_slope, precision=exact_mode)  14.4 us
  transfers between devices with their start and end apart: 5, of which 2 were waited for; matrix products, arithmetic and copies ran while one was open for 28% of the time, Pallas kernels for 0%

commit v1 on v0

--- a/solution.py
+++ b/solution.py
@@ -157,13 +157,16 @@
     point_part = jnp.einsum("crs,ors->co", field, out_slope, precision=exact_mode)
     bias_part = jnp.sum(out_slope, axis=(1, 2))
     modes_re, modes_im, point_sum, bias_sum = lax.psum(
-        (
-            widen(grad_re, C, 0),
-            widen(grad_im, C, 0),
-            widen(point_part, C, 1),
-            widen(bias_part, C, 0),
-        ),
-        ("row", "col", "ch"),
+        lax.psum(
+            (
+                widen(grad_re, C, 0),
+                widen(grad_im, C, 0),
+                widen(point_part, C, 1),
+                widen(bias_part, C, 0),
+            ),
+            ("col", "ch"),
+        ),
+        "row",
     )
     own_allowed = lax.dynamic_slice_in_dim(allowed, own_first, channel_count, 0)
     own_gre = lax.dynamic_slice_in_dim(modes_re, own_first, channel_count, 0)

time: 465 us -> 454 us (0.976)
  waiting for transfers between devices: 145 us -> 137 us
    psum x0 -> x1, blocking collectives: none -> 19.5 us  [per_device(): lax.psum(lax.psum((widen(grad_re, C, 0), widen(grad_im, C, 0), widen(poin...]
    psum x1, blocking collectives: 40.2 us -> 22.3 us  [per_device(): lax.psum((widen(grad_re, C, 0), widen(grad_im, C, 0), widen(point_part, C...]
    psum x1, waiting for transfers between devices: 55.3 us -> 46.6 us  [per_device(): lax.psum((widen(grad_re, C, 0), widen(grad_im, C, 0), widen(point_part, C...]
  transfers between devices with their start and end apart: 5 -> 6, of which waited for: 2 -> 2; matrix products, arithmetic and copies ran while one was open for 28% -> 30% of each run, Pallas kernels for 0% -> 0%
where the time goes in v1:
time: 454 us; the launch traced here: 446 us
  waiting for transfers between devices  137 us (30%)
  matrix products  127 us (28%)
  local copies, waits for them, and re-layouts  62.7 us (14%)
  other arithmetic  47.6 us (10%)
  blocking collectives  41.9 us (9%)
  starting transfers between devices  15.4 us (3%)
  between operations  14.5 us (3%)
    psum x1, waiting for transfers between devices, per_device(): lax.psum((widen(part_re, C, 0), widen(part_im, C, 0)), ('row', 'col', 'ch'))  90.1 us
    psum x1, waiting for transfers between devices, per_device(): lax.psum((widen(grad_re, C, 0), widen(grad_im, C, 0), widen(point_part, C...  46.6 us
    scatter-add x1, other arithmetic, per_device(): cotangent = jnp.zeros((channel_count, RD * CD), jnp.float32).at[:, got_ce...  26.2 us
    psum x1, blocking collectives, per_device(): lax.psum((widen(grad_re, C, 0), widen(grad_im, C, 0), widen(point_part, C...  22.3 us
    dot_general x2, matrix products, tile_field(): jnp.einsum('ar,cas->crs', sin_rows, half_im, precision=exact_mode)  21.5 us
    psum x1, blocking collectives, per_device(): lax.psum(lax.psum((widen(grad_re, C, 0), widen(grad_im, C, 0), widen(poin...  19.5 us
    reshape x1, local copies, waits for them, and re-layouts, per_device(): cotangent = cotangent.reshape(channel_count, RD, CD)  19.4 us
    dot_general x2, matrix products, tile_field(): jnp.einsum('ar,cas->crs', cos_rows, half_re, precision=exact_mode)  17 us
  transfers between devices with their start and end apart: 6, of which 2 were waited for; matrix products, arithmetic and copies ran while one was open for 30% of the time, Pallas kernels for 0%

profile of v1, /device:TPU:0, one launch (start us, length us, event | category | flops | bytes accessed | tf_op | source)
XLA Modules:
  0.0 446.3 jit_solution(15664604771785301083)
XLA Ops:
  7.9 4.5 %reduce-window.6 = s32[16,8,128]{2,1,0:T(8,128)S(1)} reduce-window(s32[16,8,128]{2,1,0:T(8,128)S(1)} %fusion.42, s32[]{:T(128)} %constant.114.clone.1), window={size=1x1x128 pad=0_0x0_0x127_0}, to_apply=%region_0.1 | reduce-window | flops 2080768 | bytes 131076 | tf_op jit(solution)/shard_map/reduce-window
  14.2 5.0 %scatter_custom_fusion = s32[2048]{0:T(1024)} fusion(s32[1024]{0:T(1024)S(1)} %bitcast.156, s32[1024]{0:T(1024)} %param.15, s32[]{:T(128)} %constant.114.clone.1), kind=kCustom, calls=%fused_computation.137 | custom fusion | bytes 8704 | tf_op jit(solution)/shard_map/scatter | solution.py:132
  19.3 8.3 %all-to-all-start = ((s32[1,16,128]{2,0,1:T(1,128)}), s32[1,16,128]{2,0,1:T(1,128)S(1)}, u32[]{:S(2)}, u32[]{:S(2)}) async-start(s32[1,16,128]{2,0,1:T(1,128)} %bitcast.7), calls=%async_computation | async-start | bytes 16384 | tf_op jit(solution)/shard_map/all_to_all | solution.py:141
  27.7 4.4 fusion.23
  32.1 4.4 fusion.17
  46.8 14.1 %fusion.4 = f32[16,128,512]{2,0,1:T(8,128)} fusion(f32[32,128,512]{2,1,0:T(8,128)} %param.8, f32[32,32]{1,0:T(8,128)S(1)} %copy-done, s32[]{:T(128)S(6)} %select_n.97), kind=kOutput, calls=%fused_computation.7 | convolution fusion | flops 402653184 | bytes 12587012 | tf_op jit(solution)/shard_map/co,crs->ors/dot_general | solution.py:119
  64.1 3.7 scatter_custom_fusion.1
  68.8 5.3 %copy.92 = f32[16,128,512]{1,2,0:T(8,128)} copy(f32[16,128,512]{2,0,1:T(8,128)} %fusion.4) | data formatting | bytes 8388608 | tf_op jit(solution)/shard_map/co,crs->ors/dot_general | solution.py:119
  74.1 7.0 %all-to-all-start.1 = ((f32[16,16,128]{2,0,1:T(8,128)}), f32[16,16,128]{2,0,1:T(8,128)}, u32[]{:S(2)}, u32[]{:S(2)}) async-start(f32[16,16,128]{2,0,1:T(8,128)} %copy.81), calls=%async_computation.1 | async-start | bytes 262144 | tf_op jit(solution)/shard_map/all_to_all | solution.py:134
  81.1 90.1 %all-reduce.9.cloned.1.call-done = (f32[32,512]{1,0:T(8,128)}, f32[32,512]{1,0:T(8,128)}) async-done(((f32[32,512]{1,0:T(8,128)}, f32[32,512]{1,0:T(8,128)}), (f32[32,512]{1,0:T(8,128)}, f32[32,512]{1,0:T(8,128)})) %all-reduce.9.cloned.1.call-update) | async-done | bytes 131088 | tf_op jit(solution)/shard_map/psum | solution.py:108
  176.2 2.3 convolution_subtract_fusion.1
  178.5 8.7 %fusion.87 = f32[16,512,128]{2,1,0:T(8,128)} fusion(f32[16,32,512]{2,1,0:T(8,128)S(1)} %convolution_subtract_fusion.1, s32[128]{0:T(128)S(1)} %iota_add_fusion.1, s32[32]{0:T(128)S(1)} %compare_select_fusion.3), kind=kOutput, calls=%fused_computation.119 | convolution fusion | flops 402710528 | bytes 5243520 | tf_op jit(solution)/shard_map/ar,cas->crs/dot_general | solution.py:88
  190.5 26.2 %scatter_custom_fusion.2 = f32[16,65536]{0,1:T(8,128)} fusion(s32[2048]{0:T(1024)S(1)} %bitcast.155, f32[2048,16]{1,0:T(8,128)S(1)} %copy.83, f32[]{:T(128)} %constant.118.clone.1), kind=kCustom, calls=%fused_computation.3 | custom fusion | flops 32768 | bytes 4194308 | tf_op jit(solution)/shard_map/scatter-add | solution.py:152
  216.7 19.4 %copy.93 = f32[16,128,512]{1,2,0:T(8,128)} copy(f32[16,128,512]{0,2,1:T(8,128)} %bitcast.147) | data formatting | bytes 8388608 | tf_op jit(solution)/shard_map/reshape | solution.py:154
  236.1 13.0 %fusion.227 = (f32[16]{0:T(128)S(1)}, f32[16,128,512]{1,2,0:T(8,128)S(1)}) fusion(f32[16,128,512]{1,2,0:T(8,128)} %copy.93, f32[16]{0:T(128)S(1)} %copy-done.14, f32[16,128,512]{1,2,0:T(8,128)} %copy.92, f32[16,512,128]{2,1,0:T(8,128)} %fusion.87, f32[16,32,512]{2,1,0:T(8,128)S(1)} %copy-done.3, s32[128]{0:T(128)S(1)} %iota_add_fusion.1, ...), kind=kOutput, calls=%fused_computation.252 | convolution fusion | flops 427876352 | bytes 17826560 | tf_op jit(solution)/shard_map/ar,cas->crs/dot_general | solution.py:88
  249.1 4.6 %fusion.26 = f32[16,32,512]{2,1,0:T(8,128)S(1)} fusion(f32[16,128,512]{1,2,0:T(8,128)S(1)} %get-tuple-element.39, s32[128]{0:T(128)S(1)} %iota_add_fusion.1, s32[32]{0:T(128)S(1)} %compare_select_fusion.3), kind=kOutput, calls=%fused_computation.31 | convolution fusion | flops 402972672 | bytes 5243520 | tf_op jit(solution)/shard_map/ar,crs->cas/dot_general | solution.py:59
  253.7 4.5 %convolution_bitcast_fusion = f32[16,32,512]{2,1,0:T(8,128)S(1)} fusion(f32[16,128,512]{1,2,0:T(8,128)S(1)} %get-tuple-element.39, s32[128]{0:T(128)S(1)} %iota_add_fusion.1, s32[32]{0:T(128)S(1)} %compare_select_fusion.3), kind=kOutput, calls=%fused_computation.32 | convolution fusion | flops 402710528 | bytes 5243520 | tf_op jit(solution)/shard_map/ar,crs->cas/dot_general | solution.py:58
  260.5 2.9 fusion.61
  263.4 2.9 fusion.30
  267.5 3.1 fusion.29
  271.6 5.9 %copy.95 = f32[16,128,512]{2,0,1:T(8,128)} copy(f32[16,128,512]{1,2,0:T(8,128)} %copy-done.1) | data formatting | bytes 8388608 | tf_op jit(solution)/shard_map/transpose(jvp())/add_any | solution.py:155
  277.6 46.6 %all-reduce.11.cloned.1.call-done = (f32[32,512]{1,0:T(8,128)}, f32[32,512]{1,0:T(8,128)}) async-done(((f32[32,512]{1,0:T(8,128)}, f32[32,512]{1,0:T(8,128)}), (f32[32,512]{1,0:T(8,128)}, f32[32,512]{1,0:T(8,128)})) %all-reduce.11.cloned.1.call-update) | async-done | bytes 131088 | tf_op jit(solution)/shard_map/psum | solution.py:160
  324.3 10.6 %fusion.77 = f32[32,128,512]{2,0,1:T(8,128)} fusion(f32[16,128,512]{2,0,1:T(8,128)} %copy.95, f32[32,32]{1,0:T(8,128)S(1)} %copy-done, s32[]{:T(128)S(6)} %select_n.97), kind=kOutput, calls=%fused_computation.109 | convolution fusion | flops 402653184 | bytes 12587012 | tf_op jit(solution)/shard_map/co,ors->crs/dot_general | solution.py:192
  335.2 14.4 %fusion.34 = f32[32,32]{0,1:T(8,128)S(1)} fusion(f32[32,32]{0,1:T(8,128)S(1)} %broadcast_in_dim.10, s32[]{:T(128)S(6)} %select_n.97, f32[16,128,512]{2,0,1:T(8,128)} %copy.95, f32[32,128,512]{2,1,0:T(8,128)} %param.8), kind=kOutput, calls=%fused_computation.46 | convolution fusion | flops 402653184 | bytes 12591108 | tf_op jit(solution)/shard_map/crs,ors->co/dot_general | solution.py:157
  349.7 22.3 %all-reduce.1 = (f32[32,32]{0,1:T(8,128)S(1)}, f32[32]{0:T(128)S(1)}) all-reduce(f32[32,32]{0,1:T(8,128)S(1)} %fusion.34, f32[32]{0:T(128)S(1)} %dynamic_update_slice.23), channel_id=1, replica_groups=mesh['row'=4,'col'=4,'ch'=2] {'col','ch'}, use_global_device_ids=true, to_apply=%region_17.18 | all-reduce | flops 1056 | bytes 8448 | tf_op jit(solution)/shard_map/psum | solution.py:160
  372.0 19.5 %all-reduce.3 = (f32[32,32]{0,1:T(8,128)S(1)}, f32[32]{0:T(128)S(1)}) all-reduce(f32[32,32]{0,1:T(8,128)S(1)} %get-tuple-element.26, f32[32]{0:T(128)S(1)} %get-tuple-element.27), channel_id=1, replica_groups=mesh['row'=4,'col'=4,'ch'=2] {'row'}, use_global_device_ids=true, to_apply=%region_18.19 | all-reduce | flops 1056 | bytes 8448 | tf_op jit(solution)/shard_map/psum | solution.py:159
  396.8 8.3 %fusion.84 = f32[16,512,128]{2,1,0:T(8,128)} fusion(f32[16,32,512]{2,1,0:T(8,128)S(1)} %convolution_subtract_fusion, s32[128]{0:T(128)S(1)} %iota_add_fusion.1, s32[32]{0:T(128)S(1)} %compare_select_fusion.3), kind=kOutput, calls=%fused_computation.116 | convolution fusion | flops 402710528 | bytes 5243520 | tf_op jit(solution)/shard_map/ar,cas->crs/dot_general | solution.py:88
  405.1 5.5 %copy.104 = f32[16,512,128]{1,0,2:T(8,128)} copy(f32[16,512,128]{2,1,0:T(8,128)} %fusion.84) | data formatting | bytes 8388608 | tf_op jit(solution)/shard_map/ar,cas->crs/dot_general | solution.py:88
  412.9 8.5 %fusion.79 = f32[16,512,128]{2,1,0:T(8,128)} fusion(f32[16,32,512]{2,1,0:T(8,128)S(1)} %convolution_add_fusion, s32[128]{0:T(128)S(1)} %iota_add_fusion.1, s32[32]{0:T(128)S(1)} %compare_select_fusion.3), kind=kOutput, calls=%fused_computation.111 | convolution fusion | flops 402710528 | bytes 5243520 | tf_op jit(solution)/shard_map/ar,cas->crs/dot_general | solution.py:88
  421.4 5.5 %copy.105 = f32[16,512,128]{1,0,2:T(8,128)} copy(f32[16,512,128]{2,1,0:T(8,128)} %fusion.79) | data formatting | bytes 8388608 | tf_op jit(solution)/shard_map/ar,cas->crs/dot_general | solution.py:88
  428.9 6.2 %bitcast_add_fusion = f32[16,128,512]{2,0,1:T(8,128)S(1)} fusion(f32[16,128,512]{2,0,1:T(8,128)} %reduce-scatter.2.cloned.1.call-done, f32[16,512,128]{1,0,2:T(8,128)} %copy.104, f32[16,512,128]{1,0,2:T(8,128)} %copy.105), kind=kLoop, calls=%fused_computation.17 | loop fusion | flops 3145728 | bytes 16777216 | tf_op jit(solution)/shard_map/add | solution.py:194
  435.1 4.4 copy.108
  (106 shorter events, 39.3 us)
Async XLA Ops:
  7.2 39.6 %copy-start = (f32[32,32]{1,0:T(8,128)S(1)}, f32[32,32]{1,0:T(8,128)}, u32[]{:S(2)}) copy-start(f32[32,32]{1,0:T(8,128)} %param.10) | copy-start | bytes 12292
  19.3 54.8 %all-to-all-start = ((s32[1,16,128]{2,0,1:T(1,128)}), s32[1,16,128]{2,0,1:T(1,128)S(1)}, u32[]{:S(2)}, u32[]{:S(2)}) async-start(s32[1,16,128]{2,0,1:T(1,128)} %bitcast.7), calls=%async_computation | async-start | bytes 16384 | tf_op jit(solution)/shard_map/all_to_all | solution.py:141
  27.6 143.7 %all-reduce.9.cloned.1.call-start = ((), (), s32[]{:S(2)}) async-start(), calls=%async_computation.4 | async-start | bytes 262144 | tf_op jit(solution)/shard_map/psum | solution.py:108
  46.1 0.6 copy-start.6
  46.1 0.6 copy-start.7
  46.8 14.2 %copy-start.13 = (s32[32]{0:T(128)S(1)}, s32[32]{0:T(128)}, u32[]{:S(2)}) copy-start(s32[32]{0:T(128)} %param.12) | copy-start | bytes 388
  46.8 14.2 %copy-start.2 = (f32[2,32,32,512]{3,2,1,0:T(8,128)S(1)}, f32[2,32,32,512]{3,2,1,0:T(8,128)}, u32[]{:S(2)}) copy-start(f32[2,32,32,512]{3,2,1,0:T(8,128)} %param.9) | copy-start | bytes 12582916
  61.0 2.1 copy-start.12
  74.1 115.2 %all-to-all-start.1 = ((f32[16,16,128]{2,0,1:T(8,128)}), f32[16,16,128]{2,0,1:T(8,128)}, u32[]{:S(2)}, u32[]{:S(2)}) async-start(f32[16,16,128]{2,0,1:T(8,128)} %copy.81), calls=%async_computation.1 | async-start | bytes 262144 | tf_op jit(solution)/shard_map/all_to_all | solution.py:134
  81.1 243.2 %all-reduce.11.cloned.1.call-start = ((), (), s32[]{:S(2)}) async-start(), calls=%async_computation.5 | async-start | bytes 262144 | tf_op jit(solution)/shard_map/psum | solution.py:160
  216.7 19.5 %copy-start.3 = (f32[16,32,512]{2,1,0:T(8,128)S(1)}, f32[16,32,512]{2,1,0:T(8,128)}, u32[]{:S(2)}) copy-start(f32[16,32,512]{2,1,0:T(8,128)} %convolution_add_fusion.1) | copy-start | bytes 3145732
  216.7 19.5 %copy-start.14 = (f32[16]{0:T(128)S(1)}, f32[16]{0:T(128)}, u32[]{:S(2)}) copy-start(f32[16]{0:T(128)} %param.11) | copy-start | bytes 196
  249.1 9.1 %copy-start.1 = (f32[16,128,512]{1,2,0:T(8,128)}, f32[16,128,512]{1,2,0:T(8,128)S(1)}, u32[]{:S(2)}) copy-start(f32[16,128,512]{1,2,0:T(8,128)S(1)} %get-tuple-element.39) | copy-start | bytes 12582916
  270.9 0.6 copy-start.8
  271.0 0.6 copy-start.9
  271.6 121.1 %all-reduce.13.cloned.1.call-start = ((), (), s32[]{:S(2)}) async-start(), calls=%async_computation.6 | async-start | bytes 262144 | tf_op jit(solution)/shard_map/psum | solution.py:159
  324.2 104.6 %reduce-scatter.2.cloned.1.call-start = ((), (), s32[]{:S(2)}) async-start(), calls=%async_computation.3 | async-start | bytes 12582912 | tf_op jit(solution)/shard_map/reduce_scatter | solution.py:193
  421.4 5.6 %copy-start.11 = (f32[32,512]{1,0:T(8,128)S(1)}, f32[32,512]{1,0:T(8,128)}, u32[]{:S(2)}) copy-start(f32[32,512]{1,0:T(8,128)} %get-tuple-element.32) | copy-start | bytes 196612
  421.4 5.6 %copy-start.10 = (f32[32,512]{1,0:T(8,128)S(1)}, f32[32,512]{1,0:T(8,128)}, u32[]{:S(2)}) copy-start(f32[32,512]{1,0:T(8,128)} %get-tuple-element.33) | copy-start | bytes 196612
  421.4 5.6 %copy-start.4 = (f32[32,512]{1,0:T(8,128)S(1)}, f32[32,512]{1,0:T(8,128)}, u32[]{:S(2)}) copy-start(f32[32,512]{1,0:T(8,128)} %get-tuple-element.24) | copy-start | bytes 196612
  421.4 5.6 %copy-start.5 = (f32[32,512]{1,0:T(8,128)S(1)}, f32[32,512]{1,0:T(8,128)}, u32[]{:S(2)}) copy-start(f32[32,512]{1,0:T(8,128)} %get-tuple-element.25) | copy-start | bytes 196612
Sparse Core Ops, SparseCore 0:
  46.9 124.3 all-reduce.8
  271.7 52.4 all-reduce.10
  326.7 33.9 all-reduce.12
  362.8 16.4 reduce-scatter.1
